TPU v7x, 128 devices: a whole 4x4x4 slice. The times are simulated.
128 devices in a mesh: gen: 8 (over y_hi, x), dom: 8 (over z, y_lo), dp: 2 (over core).
Axes of the slice: x: 4, y: 4 (y_hi: 2, y_lo: 2; y = y_hi * 2 + y_lo), z: 4, core: 2. Of those that a mesh axis runs over, the one named last changes fastest.
Arguments:
- gen_hidden: bfloat16 [2048, 4096], P(('dp', 'dom'), 'gen'), parts along dimension 0, may hold values from -52 to 52
- gen_gain: float32 [8192], P('dp'), parts along dimension 0, may hold values from 0.25 to 1.75
- gen_head: bfloat16 [131072, 4096], P(('dp', 'gen', 'dom')), parts along dimension 0, may hold values from -24 to 24
- dom_hidden: bfloat16 [2048, 4096], P(('dp', 'gen'), 'dom'), parts along dimension 0, may hold values from -52 to 52
- dom_gain: float32 [8192], P('dp'), parts along dimension 0, may hold values from 0.25 to 1.75
- dom_head: bfloat16 [131072, 4096], P(('dp', 'gen', 'dom')), parts along dimension 0, may hold values from -24 to 24
- targets: int32 [2048], P('dp'), parts along dimension 0, may hold values from 0 to 65535
- doc_ids: int32 [2048], P('dp'), parts along dimension 0, may hold values from -1 to 63, as said below
Outputs:
- token_diff: float32 [2048], P(('dp', 'dom')), parts along dimension 0
- doc_score: float32 [128], P(('dp', 'dom')), parts along dimension 0
There are 2 independent parts, one for each index of `dp`. A program takes and returns all parts, laid end to end along the dimension named above; each array names one. Nothing has to cross between parts.
Inputs may be any that keep to these rules, and one draw needn't show every extreme that they name: `doc_ids`: rows 128 * p to 128 * p + 127 form pack p. Each pack begins with rows of exactly 8 documents, numbered 8 * p onwards in order, each one row or more, and ends with padding rows marked -1. The packs fall into pairs whose document rows add up to 136, so the batch holds 544 document rows, and some pack has no padding.
All inputs are finite; a program needn't handle non-finite values.
Results may differ from a plain program's by a relative error of at most 0.0045.
Values may be sent and summed in bfloat16 or wider, within the bound.
A program may use at most 128 MiB of HBM per device.

v0:
```python
import jax
import jax.numpy as jnp
from jax import lax
from jax.sharding import PartitionSpec as P

DOC_PACK = 8


def joined(shard, axis, combine):
    everything = jax.tree.map(lambda part: lax.all_gather(part, axis), shard)
    first = jax.tree.map(lambda part: part[0], everything)

    def turn(k, so_far):
        return combine(so_far, jax.tree.map(lambda part: part[k], everything))

    return lax.fori_loop(1, lax.axis_size(axis), turn, first)


def scale_rows(values_bf, scaling, sum_axes, full_width):
    values = values_bf.astype(jnp.float32)
    meansq = jnp.sum(values * values, axis=sum_axes, keepdims=True) / full_width
    return (values * lax.rsqrt(meansq + 1e-05) * scaling).astype(jnp.bfloat16)


def row_stats(logits, wanted):
    highest = jnp.max(logits, axis=1)
    exp_total = jnp.sum(jnp.exp(logits - highest[:, None]), axis=1)
    columns = lax.broadcasted_iota(jnp.int32, logits.shape, 1)
    picked = jnp.sum(jnp.where(columns == wanted[:, None], logits, 0.0), axis=1)
    return (highest, exp_total, picked)


def combine(former, latter):
    highest = jnp.maximum(former[0], latter[0])
    exp_total = former[1] * jnp.exp(former[0] - highest) + latter[1] * jnp.exp(latter[0] - highest)
    return (highest, exp_total, former[2] + latter[2])


def general_stats(gen_hidden, gen_gain, gen_head, wanted_all):
    rows_dev, width_dev = gen_hidden.shape
    full_width = gen_gain.shape[0]
    gen_count = lax.axis_size("gen")
    dom_count = lax.axis_size("dom")
    block_rows = gen_head.shape[0]
    rows_all = rows_dev * dom_count
    blocks = lax.all_gather(gen_hidden[None], ("gen", "dom"), axis=0, tiled=True)
    blocks = blocks.reshape(gen_count, rows_all, width_dev)
    gain_blocks = gen_gain.reshape(gen_count, 1, width_dev)
    head_blocks = gen_head.reshape(block_rows, gen_count, width_dev)
    normed = scale_rows(blocks, gain_blocks, (0, 2), full_width)
    logits = lax.dot_general(
        normed, head_blocks, (((0, 2), (1, 2)), ((), ())), preferred_element_type=jnp.float32
    )
    row_totals = row_stats(logits, wanted_all)
    highest, exp_total, picked = joined(row_totals, ("gen", "dom"), combine)
    return picked - (highest + jnp.log(exp_total))


def domain_stats(dom_hidden, dom_gain, dom_head, wanted_all):
    rows_dev, width_dev = dom_hidden.shape
    full_width = dom_gain.shape[0]
    gen_count = lax.axis_size("gen")
    dom_count = lax.axis_size("dom")
    block_rows = dom_head.shape[0]
    rows_all = rows_dev * gen_count
    blocks = lax.all_gather(dom_hidden[None], ("gen", "dom"), axis=0, tiled=True)
    blocks = blocks.reshape(gen_count, dom_count, rows_dev, width_dev)
    head_blocks = dom_head.reshape(block_rows, dom_count, width_dev)
    gain_blocks = dom_gain.reshape(1, dom_count, 1, width_dev)
    normed = scale_rows(blocks, gain_blocks, (1, 3), full_width)
    logits = lax.dot_general(
        normed, head_blocks, (((1, 3), (1, 2)), ((), ())), preferred_element_type=jnp.float32
    )
    row_totals = row_stats(logits.reshape(rows_all, block_rows), wanted_all)
    highest, exp_total, picked = joined(row_totals, ("gen", "dom"), combine)
    return picked - (highest + jnp.log(exp_total))


def per_device(gen_hidden, gen_gain, gen_head, dom_hidden, dom_gain, dom_head, targets, doc_ids):
    rows_dev = gen_hidden.shape[0]
    first_column = (
        lax.axis_index("gen") * lax.axis_size("dom") + lax.axis_index("dom")
    ) * gen_head.shape[0]
    wanted_all = targets - first_column
    gen_logprob = general_stats(gen_hidden, gen_gain, gen_head, wanted_all)
    dom_logprob = domain_stats(dom_hidden, dom_gain, dom_head, wanted_all)
    is_live = doc_ids >= 0
    token_all = jnp.where(is_live, dom_logprob - gen_logprob, 0.0)
    pack_index = lax.axis_index("dom")
    token_own = lax.dynamic_slice_in_dim(token_all, pack_index * rows_dev, rows_dev)
    docs_own = (
        lax.dynamic_slice_in_dim(doc_ids, pack_index * rows_dev, rows_dev) - pack_index * DOC_PACK
    )
    onehot = (docs_own[:, None] == jnp.arange(DOC_PACK, dtype=jnp.int32)[None, :]).astype(
        jnp.float32
    )
    doc_sums = jnp.dot(token_own, onehot, precision=lax.Precision.HIGHEST)
    counts = jnp.sum(onehot, axis=0)
    return (token_own, doc_sums / counts)


def solution(mesh):
    in_specs = (
        P(("dp", "dom"), "gen"),
        P("dp"),
        P(("dp", "gen", "dom"), None),
        P(("dp", "gen"), "dom"),
        P("dp"),
        P(("dp", "gen", "dom"), None),
        P("dp"),
        P("dp"),
    )
    out_specs = (P(("dp", "dom")), P(("dp", "dom")))
    return jax.shard_map(
        per_device, mesh=mesh, in_specs=in_specs, out_specs=out_specs, check_vma=False
    )
```

profile of v0, /device:TPU:8, one launch (start us, length us, event | category | flops | bytes accessed | tf_op | source)
XLA Modules:
  0.0 1784.5 jit_solution(5406152321257120198)
XLA Ops:
  7.2 0.0 all-gather.11.cloned.1.call-start
  7.2 0.7 all-gather.11.cloned.1.call-update
  7.9 0.0 all-gather.13.cloned.1.call-start
  7.9 0.7 all-gather.13.cloned.1.call-update
  8.7 0.7 mul.110
  9.4 0.7 mul.120
  10.1 0.8 dynamic-slice_subtract_fusion
  10.9 0.1 convert_reduce_fusion
  11.0 0.7 broadcast_subtract_fusion
  11.7 340.2 %all-gather.11.cloned.1.call-done = bf16[8192,512]{1,0:T(8,128)(2,1)} async-done(((bf16[128,512]{1,0:T(8,128)(2,1)}), bf16[8192,512]{1,0:T(8,128)(2,1)}) %all-gather.11.cloned.1.call-update) | async-done | bytes 8388624 | tf_op jit(solution)/shard_map/all_gather | solution.py:66
  351.9 5.1 multiply_reduce_fusion
  357.1 9.4 fusion.3
  366.4 7.6 copy.16
  374.0 321.7 %all-gather.13.cloned.1.call-done = bf16[8192,512]{1,0:T(8,128)(2,1)} async-done(((bf16[128,512]{1,0:T(8,128)(2,1)}), bf16[8192,512]{1,0:T(8,128)(2,1)}) %all-gather.13.cloned.1.call-update) | async-done | bytes 8388624 | tf_op jit(solution)/shard_map/all_gather | solution.py:46
  695.7 5.1 fusion
  700.9 0.0 copy-start
  700.9 13.2 bitcast_reduce_fusion.1
  714.1 0.0 copy-done
  714.2 2.5 fusion.2
  716.6 11.3 bitcast_reduce_fusion
  727.9 0.0 copy-start.1
  727.9 2.0 fusion.15
  729.9 173.9 %all-gather.2 = f32[65536]{0:T(1024)S(1)} all-gather(f32[1024]{0:T(1024)S(1)} %get-tuple-element.365), channel_id=4, replica_groups=mesh['gen'=8,'dom'=8,'dp'=2] {'gen','dom'}, dimensions={0}, use_global_device_ids=true | all-gather | bytes 266240 | tf_op jit(solution)/shard_map/all_gather | solution.py:10
  903.9 174.6 %all-gather.3 = f32[65536]{0:T(1024)S(1)} all-gather(f32[1024]{0:T(1024)S(1)} %get-tuple-element.364), channel_id=5, replica_groups=mesh['gen'=8,'dom'=8,'dp'=2] {'gen','dom'}, dimensions={0}, use_global_device_ids=true | all-gather | bytes 266240 | tf_op jit(solution)/shard_map/all_gather | solution.py:10
  1078.6 170.6 %all-gather.1 = f32[65536]{0:T(1024)S(1)} all-gather(f32[1024]{0:T(1024)S(1)} %get-tuple-element.408), channel_id=3, replica_groups=mesh['gen'=8,'dom'=8,'dp'=2] {'gen','dom'}, dimensions={0}, use_global_device_ids=true | all-gather | bytes 266240 | tf_op jit(solution)/shard_map/all_gather | solution.py:10
  1249.3 172.5 %all-gather.6 = f32[65536]{0:T(1024)S(1)} all-gather(f32[1024]{0:T(1024)S(1)} %get-tuple-element.368), channel_id=8, replica_groups=mesh['gen'=8,'dom'=8,'dp'=2] {'gen','dom'}, dimensions={0}, use_global_device_ids=true | all-gather | bytes 266240 | tf_op jit(solution)/shard_map/all_gather | solution.py:10
  1421.8 170.6 %all-gather.7 = f32[65536]{0:T(1024)S(1)} all-gather(f32[1024]{0:T(1024)S(1)} %get-tuple-element.369), channel_id=9, replica_groups=mesh['gen'=8,'dom'=8,'dp'=2] {'gen','dom'}, dimensions={0}, use_global_device_ids=true | all-gather | bytes 266240 | tf_op jit(solution)/shard_map/all_gather | solution.py:10
  1592.5 172.5 %all-gather.5 = f32[65536]{0:T(1024)S(1)} all-gather(f32[1024]{0:T(1024)S(1)} %get-tuple-element.406), channel_id=7, replica_groups=mesh['gen'=8,'dom'=8,'dp'=2] {'gen','dom'}, dimensions={0}, use_global_device_ids=true | all-gather | bytes 266240 | tf_op jit(solution)/shard_map/all_gather | solution.py:10
  1765.1 5.9 while.38
  1771.0 5.9 while.39
  1776.9 0.0 copy-done.1
  1776.9 0.1 dynamic_slice.66
  1777.0 0.0 copy-start.2
  1777.0 0.6 fusion.16
  1777.6 0.0 copy-done.2
  (524 shorter events, 6.0 us)
Async XLA Ops:
  7.2 344.8 %all-gather.11.cloned.1.call-start = ((), (), s32[]{:S(2)}) async-start(), calls=%async_computation | async-start | bytes 8519680 | tf_op jit(solution)/shard_map/all_gather | solution.py:66
  7.9 687.8 %all-gather.13.cloned.1.call-start = ((), (), s32[]{:S(2)}) async-start(), calls=%async_computation.1 | async-start | bytes 8519680 | tf_op jit(solution)/shard_map/all_gather | solution.py:46
  700.9 13.2 copy-start
  727.9 1049.0 %copy-start.1 = (s32[1024]{0:T(1024)S(1)}, s32[1024]{0:T(1024)}, u32[]{:S(2)}) copy-start(s32[1024]{0:T(1024)} %param.19) | copy-start | bytes 12292
  1777.0 0.6 copy-start.2
Sparse Core Ops, SparseCore 0:
  9.6 342.2 all-gather.10
  353.6 342.1 all-gather.12
where the time goes:
time: 1780 us
  blocking collectives  1030 us (58%)
  waiting for transfers between devices  663 us (37%)
  other arithmetic  27.7 us (2%)
  matrix products  25.1 us (1%)
    all_gather x6, blocking collectives, joined(): everything = jax.tree.map(lambda part: lax.all_gather(part, axis), shard)  1030 us
    all_gather x1, waiting for transfers between devices, domain_stats(): lax.all_gather(dom_hidden[None], ('gen', 'dom'), axis=0, tiled=True)  340 us
    all_gather x1, waiting for transfers between devices, general_stats(): lax.all_gather(gen_hidden[None], ('gen', 'dom'), axis=0, tiled=True)  322 us
  transfers between devices with their start and end apart: 2, of which 2 were waited for; matrix products, arithmetic and copies ran while one was open for 1% of the time, Pallas kernels for 0%

commit v1 on v0

--- a/solution.py
+++ b/solution.py
@@ -43,7 +43,12 @@
     dom_count = lax.axis_size("dom")
     block_rows = gen_head.shape[0]
     rows_all = rows_dev * dom_count
-    blocks = lax.all_gather(gen_hidden[None], ("gen", "dom"), axis=0, tiled=True)
+    blocks = jnp.concatenate(
+        lax.all_to_all(
+            jnp.stack([gen_hidden[None]] * lax.axis_size(("gen", "dom"))), ("gen", "dom"), 0, 0
+        ),
+        axis=0,
+    )
     blocks = blocks.reshape(gen_count, rows_all, width_dev)
     gain_blocks = gen_gain.reshape(gen_count, 1, width_dev)
     head_blocks = gen_head.reshape(block_rows, gen_count, width_dev)

time: 1780 us -> 1370 us (0.77)
  waiting for transfers between devices: 663 us -> 226 us
    all_gather x1 -> x0, waiting for transfers between devices: 322 us -> none  [general_stats(): lax.all_gather(gen_hidden[None], ('gen', 'dom'), axis=0, tiled=True)]
    all_gather x1, waiting for transfers between devices: 340 us -> 93.6 us  [domain_stats(): lax.all_gather(dom_hidden[None], ('gen', 'dom'), axis=0, tiled=True)]
    all_to_all x0 -> x1, waiting for transfers between devices: none -> 132 us  [general_stats(): lax.all_to_all(jnp.stack([gen_hidden[None]] * lax.axis_size(('gen', 'dom'...]
  transfers between devices with their start and end apart: 2 -> 2, of which waited for: 2 -> 2; matrix products, arithmetic and copies ran while one was open for 1% -> 2% of each run, Pallas kernels for 0% -> 0%
where the time goes in v1:
time: 1370 us
  blocking collectives  1030 us (75%)
  waiting for transfers between devices  226 us (16%)
  other arithmetic  29.2 us (2%)
  matrix products  26.2 us (2%)
  local copies, waits for them, and re-layouts  16.8 us (1%)
  between operations  14.3 us (1%)
    all_gather x6, blocking collectives, joined(): everything = jax.tree.map(lambda part: lax.all_gather(part, axis), shard)  1030 us
    all_to_all x1, waiting for transfers between devices, general_stats(): lax.all_to_all(jnp.stack([gen_hidden[None]] * lax.axis_size(('gen', 'dom'...  132 us
    all_gather x1, waiting for transfers between devices, domain_stats(): lax.all_gather(dom_hidden[None], ('gen', 'dom'), axis=0, tiled=True)  93.6 us
  transfers between devices with their start and end apart: 2, of which 2 were waited for; matrix products, arithmetic and copies ran while one was open for 2% of the time, Pallas kernels for 0%

profile of v1, /device:TPU:8, one launch (start us, length us, event | category | flops | bytes accessed | tf_op | source)
XLA Modules:
  0.0 1365.1 jit_solution(7607980228907119046)
XLA Ops:
  7.2 0.0 all-gather.9.cloned.1.call-start
  7.2 0.7 all-gather.9.cloned.1.call-update
  7.9 5.1 stack.3
  13.0 0.0 copy-start.2
  13.0 0.0 copy-start.3
  13.0 0.0 copy-start.4
  13.0 0.0 copy-start.5
  13.0 11.7 all-to-all-start
  24.8 0.0 copy-done.2
  24.8 0.0 copy-done.3
  24.9 0.0 copy-done.4
  24.9 0.1 dynamic-slice_subtract_fusion
  24.9 0.1 convert_reduce_fusion
  25.1 0.0 copy-done.5
  25.1 131.8 %all-to-all-done = bf16[64,1,128,512]{3,2,1,0:T(8,128)(2,1)} async-done(((bf16[64,1,128,512]{3,2,1,0:T(8,128)(2,1)}), bf16[64,1,128,512]{3,2,1,0:T(8,128)(2,1)}, u32[]{:S(2)}, u32[]{:S(2)}) %all-to-all-start) | async-done | bytes 8388640 | tf_op jit(solution)/shard_map/all_to_all | solution.py:47
  156.9 5.1 fusion
  162.1 5.3 fusion.2
  167.4 12.6 bitcast_reduce_fusion
  180.0 172.3 %all-gather.4 = f32[65536]{0:T(1024)S(1)} all-gather(f32[1024]{0:T(1024)S(1)} %get-tuple-element.406), channel_id=6, replica_groups=mesh['gen'=8,'dom'=8,'dp'=2] {'gen','dom'}, dimensions={0}, use_global_device_ids=true | all-gather | bytes 266240 | tf_op jit(solution)/shard_map/all_gather | solution.py:10
  352.3 0.0 copy-start.1
  352.3 93.6 %all-gather.9.cloned.1.call-done = bf16[8192,512]{1,0:T(8,128)(2,1)} async-done(((bf16[128,512]{1,0:T(8,128)(2,1)}), bf16[8192,512]{1,0:T(8,128)(2,1)}) %all-gather.9.cloned.1.call-update) | async-done | bytes 8388624 | tf_op jit(solution)/shard_map/all_gather | solution.py:71
  445.9 5.1 multiply_reduce_fusion
  451.1 9.4 fusion.3
  460.4 0.0 copy-done.1
  460.4 7.6 copy.16
  468.0 0.0 copy-start
  468.0 13.0 bitcast_reduce_fusion.1
  481.0 0.0 slice-start
  481.0 0.0 copy-done
  481.1 2.0 fusion.15
  483.1 174.1 %all-gather.2 = f32[65536]{0:T(1024)S(1)} all-gather(f32[1024]{0:T(1024)S(1)} %get-tuple-element.365), channel_id=4, replica_groups=mesh['gen'=8,'dom'=8,'dp'=2] {'gen','dom'}, dimensions={0}, use_global_device_ids=true | all-gather | bytes 266240 | tf_op jit(solution)/shard_map/all_gather | solution.py:10
  657.2 174.5 %all-gather.3 = f32[65536]{0:T(1024)S(1)} all-gather(f32[1024]{0:T(1024)S(1)} %get-tuple-element.364), channel_id=5, replica_groups=mesh['gen'=8,'dom'=8,'dp'=2] {'gen','dom'}, dimensions={0}, use_global_device_ids=true | all-gather | bytes 266240 | tf_op jit(solution)/shard_map/all_gather | solution.py:10
  831.7 170.6 %all-gather.1 = f32[65536]{0:T(1024)S(1)} all-gather(f32[1024]{0:T(1024)S(1)} %get-tuple-element.408), channel_id=3, replica_groups=mesh['gen'=8,'dom'=8,'dp'=2] {'gen','dom'}, dimensions={0}, use_global_device_ids=true | all-gather | bytes 266240 | tf_op jit(solution)/shard_map/all_gather | solution.py:10
  1002.4 172.6 %all-gather.5 = f32[65536]{0:T(1024)S(1)} all-gather(f32[1024]{0:T(1024)S(1)} %get-tuple-element.368), channel_id=7, replica_groups=mesh['gen'=8,'dom'=8,'dp'=2] {'gen','dom'}, dimensions={0}, use_global_device_ids=true | all-gather | bytes 266240 | tf_op jit(solution)/shard_map/all_gather | solution.py:10
  1175.0 170.6 %all-gather.6 = f32[65536]{0:T(1024)S(1)} all-gather(f32[1024]{0:T(1024)S(1)} %get-tuple-element.369), channel_id=8, replica_groups=mesh['gen'=8,'dom'=8,'dp'=2] {'gen','dom'}, dimensions={0}, use_global_device_ids=true | all-gather | bytes 266240 | tf_op jit(solution)/shard_map/all_gather | solution.py:10
  1345.7 5.9 while.38
  1351.6 0.0 slice-done
  1351.6 5.9 while.39
  1357.5 0.1 dynamic_slice.66
  1357.6 0.0 copy-start.6
  1357.6 0.6 fusion.16
  1358.2 0.0 copy-done.6
  (526 shorter events, 6.0 us)
Async XLA Ops:
  7.2 438.8 %all-gather.9.cloned.1.call-start = ((), (), s32[]{:S(2)}) async-start(), calls=%async_computation.1 | async-start | bytes 8519680 | tf_op jit(solution)/shard_map/all_gather | solution.py:71
  13.0 11.8 copy-start.2
  13.0 11.8 copy-start.3
  13.0 11.8 copy-start.4
  13.0 12.0 copy-start.5
  13.0 143.9 %all-to-all-start = ((bf16[64,1,128,512]{3,2,1,0:T(8,128)(2,1)}), bf16[64,1,128,512]{3,2,1,0:T(8,128)(2,1)}, u32[]{:S(2)}, u32[]{:S(2)}) async-start(bf16[64,1,128,512]{3,2,1,0:T(8,128)(2,1)} %stack.3), calls=%async_computation | async-start | bytes 16777216 | tf_op jit(solution)/shard_map/all_to_all | solution.py:47
  352.3 108.1 %copy-start.1 = (f32[65536]{0:T(1024)}, f32[65536]{0:T(1024)S(1)}, u32[]{:S(2)}) copy-start(f32[65536]{0:T(1024)S(1)} %all-gather.4) | copy-start | bytes 786436
  468.0 13.0 copy-start
  481.0 870.5 %slice-start = ((f32[65536]{0:T(1024)}), f32[1024]{0:T(1024)S(1)}, s32[]{:S(2)}) async-start(f32[65536]{0:T(1024)} %copy-done.1), calls=%async_computation.2 | async-start | bytes 8192 | tf_op jit(solution)/shard_map/slice | solution.py:11
  1357.6 0.6 copy-start.6
Sparse Core Ops, SparseCore 0:
  9.6 436.2 all-gather.8
